TPU v7x, 32 devices: a whole 2x2x4 slice. The times are simulated.
32 devices in a mesh: fsdp: 4 (over y, core), ctx: 8 (over z, x).
Axes of the slice: x: 2, y: 2, z: 4, core: 2. Of those that a mesh axis runs over, the one named last changes fastest.
Arguments:
- token_ids: int32 [2048], P('ctx'), may hold values from 0 to 15
- table: float32 [16, 4096], P(None, 'fsdp'), may hold values from -6 to 6
- norm_gain: float32 [4096], P('fsdp'), may hold values from 0.25 to 1.75
- conv_weight: float32 [4, 4096], P(None, 'fsdp'), may hold values from -4 to 4
- conv_bias: float32 [4096], P('fsdp'), may hold values from -4 to 4
- weight_b: bfloat16 [4096, 128], P('fsdp'), may hold values from -0.09375 to 0.09375
- weight_c: bfloat16 [4096, 128], P('fsdp'), may hold values from -0.09375 to 0.09375
- step_weight: bfloat16 [4096, 64], P('fsdp'), may hold values from -0.1875 to 0.1875
- step_bias: float32 [64], P('fsdp'), as said below
- log_rate: float32 [64], P('fsdp'), as said below
- skip_gain: float32 [64], P('fsdp'), may hold values from 0.25 to 1.75
- out_grad: bfloat16 [2048, 4096], P('ctx', 'fsdp'), may hold values from -6 to 6
Outputs:
- mixer_out: bfloat16 [2048, 4096], P('ctx', 'fsdp')
- grad_embedded: bfloat16 [2048, 4096], P('ctx', 'fsdp')
- grad_table: float32 [16, 4096], P(None, 'fsdp')
- grad_norm_gain: float32 [4096], P('fsdp')
- grad_conv_weight: float32 [4, 4096], P(None, 'fsdp')
- grad_conv_bias: float32 [4096], P('fsdp')
- grad_weight_b: float32 [4096, 128], P('fsdp')
- grad_weight_c: float32 [4096, 128], P('fsdp')
- grad_step_weight: float32 [4096, 64], P('fsdp')
- grad_step_bias: float32 [64], P('fsdp')
- grad_log_rate: float32 [64], P('fsdp')
- grad_skip_gain: float32 [64], P('fsdp')
Inputs may be any that keep to these rules, and one draw needn't show every extreme that they name: exp(log_rate) lies between 1 / 16 and 1 for every head. step_bias lies between log(1 / 2048) - 1 and log(0.2) - 1.
All inputs are finite; a program needn't handle non-finite values.
Results may differ from a plain program's by a relative error of at most 0.02.
Values may be sent and summed in bfloat16 or wider, within the bound.
A program may use at most 128 MiB of HBM per device.

v0:
```python
import functools

import jax
import jax.numpy as jnp
from jax import lax
from jax.experimental import pallas as pl
from jax.experimental.pallas import tpu as pltpu
from jax.sharding import PartitionSpec as P

F32 = jnp.float32
BF = jnp.bfloat16
HI = lax.Precision.HIGHEST
VMEM_LIMIT = 56 * 1024 * 1024


def dot(a, b, ca=1, cb=0, precision=None):
    return lax.dot_general(
        a, b, (((ca,), (cb,)), ((), ())), precision=precision, preferred_element_type=F32
    )


def split_dot(value, sel, cb=0):
    hi = value.astype(BF)
    lo = (value - hi.astype(F32)).astype(BF)
    return dot(hi, sel, 1, cb) + dot(lo, sel, 1, cb)


def softplus(v):
    return jnp.maximum(v, 0.0) + jnp.log1p(jnp.exp(-jnp.abs(v)))


def selector(heads, width):
    per = width // heads
    row = lax.broadcasted_iota(jnp.int32, (heads, width), 0)
    col = lax.broadcasted_iota(jnp.int32, (heads, width), 1)
    return jnp.where((col >= row * per) & (col < row * per + per), 1.0, 0.0).astype(BF)


def order_mask(rows, reverse):
    t = lax.broadcasted_iota(jnp.int32, (rows, rows), 0)
    s = lax.broadcasted_iota(jnp.int32, (rows, rows), 1)
    return (s >= t) if reverse else (s <= t)


def whole_kernel(fn, outs, args):
    count = len(args)

    def body(*refs):
        results = fn(*[r[...] for r in refs[:count]])
        for ref, value in zip(refs[count:], results):
            ref[...] = value.astype(ref.dtype)

    return pl.pallas_call(
        body,
        out_shape=tuple(jax.ShapeDtypeStruct(s, d) for s, d in outs),
        compiler_params=pltpu.CompilerParams(vmem_limit_bytes=VMEM_LIMIT),
    )(*args)


def states_stage(raw_f, raw_r, bias, log_rate, xf, xr, bf, cf, br, cr, dy):
    rows, heads = raw_f.shape
    sel = selector(heads, xf.shape[1])
    rate = jnp.exp(log_rate)
    cols = []
    states = []
    dstates = []
    for raw, x, b, c, reverse in ((raw_f, xf, bf, cf, False), (raw_r, xr, br, cr, True)):
        step = softplus(raw + bias)
        logdec = -step * rate
        tri = jnp.where(order_mask(rows, reverse), 1.0, 0.0)
        cumul = dot(tri, logdec, precision=HI)
        end = jnp.sum(logdec, axis=0, keepdims=True)
        wt = jnp.exp(end - cumul) * step
        xs = (split_dot(wt, sel) * x.astype(F32)).astype(BF)
        states.append(dot(b, xs, 0, 0))
        gy = (split_dot(jnp.exp(cumul), sel) * dy.astype(F32)).astype(BF)
        dstates.append(dot(c, gy, 0, 0))
        cols += [cumul, step, end]
    return (
        jnp.stack(states + dstates),
        cols[0],
        cols[1],
        cols[2],
        cols[3],
        cols[4],
        cols[5],
    )


def intra_kernel(cols_ref, cut_ref, xf_ref, xr_ref, dy_ref, bf_ref, cf_ref, br_ref, cr_ref,
                 yf_ref, yr_ref, pf_ref, pr_ref, df_ref, dr_ref, inner_f, inner_r):
    rows = xf_ref.shape[0]
    per = xf_ref.shape[1] // 2

    @pl.when(pl.program_id(0) == 0)
    def _():
        inner_f[...] = dot(cf_ref[...], bf_ref[...], 1, 1)
        inner_r[...] = dot(cr_ref[...], br_ref[...], 1, 1)
        df_ref[...] = jnp.zeros_like(df_ref)
        dr_ref[...] = jnp.zeros_like(dr_ref)

    dy = dy_ref[...]
    lane = lax.broadcasted_iota(jnp.int32, dy.shape, 1)
    zero = jnp.zeros_like(dy)
    cols = cols_ref[0]
    cut = cut_ref[0]
    for branch, (x_ref, inner, y_ref, p_ref, d_ref) in enumerate(
        ((xf_ref, inner_f, yf_ref, pf_ref, df_ref), (xr_ref, inner_r, yr_ref, pr_ref, dr_ref))
    ):
        mask = order_mask(rows, branch == 1)
        st = jnp.where(
            lane < per,
            cols[:, 4 + 2 * branch : 5 + 2 * branch],
            cols[:, 5 + 2 * branch : 6 + 2 * branch],
        )
        xs = (st * x_ref[...].astype(F32)).astype(BF)
        y = None
        p = None
        total = d_ref[...]
        for k in range(2):
            mine = (lane < per) if k == 0 else (lane >= per)
            at = 2 * branch + k
            spread = cols[:, at : at + 1] - cut[at : at + 1, :]
            decay = jnp.exp(jnp.where(mask, spread, -1e30))
            mixing = (inner[...] * decay).astype(BF)
            xs_k = jnp.where(mine, xs, zero)
            dy_k = jnp.where(mine, dy, zero)
            y_k = dot(mixing, xs_k)
            p_k = dot(mixing, dy_k, 0, 0)
            total = total + dot(dy, xs_k, 1, 1) * decay
            y = y_k if y is None else y + y_k
            p = p_k if p is None else p + p_k
        y_ref[...] = y
        p_ref[...] = p
        d_ref[...] = total


def intra_stage(cols, cut, xf, xr, dy, bf, cf, br, cr):
    rows, width = xf.shape
    pairs = cols.shape[0]
    lanes = width // pairs
    wide = pl.BlockSpec((rows, lanes), lambda j: (0, j))
    small = pl.BlockSpec(bf.shape, lambda j: (0, 0))
    square = pl.BlockSpec((rows, rows), lambda j: (0, 0))
    return pl.pallas_call(
        intra_kernel,
        grid=(pairs,),
        in_specs=[
            pl.BlockSpec((1, rows, 8), lambda j: (j, 0, 0)),
            pl.BlockSpec((1, 4, rows), lambda j: (j, 0, 0)),
            wide,
            wide,
            wide,
            small,
            small,
            small,
            small,
        ],
        out_specs=[wide, wide, wide, wide, square, square],
        out_shape=[jax.ShapeDtypeStruct((rows, width), F32)] * 4
        + [jax.ShapeDtypeStruct((rows, rows), F32)] * 2,
        scratch_shapes=[pltpu.VMEM((rows, rows), F32), pltpu.VMEM((rows, rows), F32)],
        compiler_params=pltpu.CompilerParams(vmem_limit_bytes=VMEM_LIMIT),
    )(cols, cut, xf, xr, dy, bf, cf, br, cr)


def joined_stage(chained, yf, yr, pf, pr, df, dr, xf, xr, dy_half, bf, cf, br, cr,
                 raw_f, raw_r, cum_f, cum_r, bias, log_rate, skip):
    rows, heads = raw_f.shape
    sel = selector(heads, xf.shape[1])
    rate = jnp.exp(log_rate)
    dy = dy_half.astype(F32)
    channel = split_dot(jnp.broadcast_to(skip, (8, heads)), sel)[:1]
    both = xf.astype(F32) + xr.astype(F32)
    mixed = channel * both
    direct = channel * dy
    d_skip = jnp.sum(split_dot(dy * both, sel, 1), axis=0, keepdims=True)
    results = []
    d_bias = 0.0
    d_rate = 0.0
    for k, (intra, p, square, x_half, b, c, raw, cumul) in enumerate(
        ((yf, pf, df, xf, bf, cf, raw_f, cum_f), (yr, pr, dr, xr, br, cr, raw_r, cum_r))
    ):
        reverse = k == 1
        start = chained[k]
        leaving = chained[2 + k]
        x = x_half.astype(F32)
        shifted = raw + bias
        step = softplus(shifted)
        logdec = -step * rate
        end = jnp.sum(logdec, axis=0, keepdims=True)
        grow = split_dot(jnp.exp(cumul), sel)
        fade = split_dot(jnp.exp(end - cumul), sel)
        wide_step = split_dot(step, sel)
        start_half = start.astype(BF)
        leaving_half = leaving.astype(BF)
        y = intra + grow * dot(c, start_half)
        mixed = mixed + y
        state_back = fade * dot(b, leaving_half)
        q = p + state_back
        x_step = wide_step * x
        d_x = wide_step * q + direct
        square_half = square.astype(BF)
        gy = (grow * dy).astype(BF)
        d_c = dot(square_half, b) + dot(gy, start_half, 1, 1)
        xs2 = (x_step * fade).astype(BF)
        d_b = dot(square_half, c, 0, 0) + dot(xs2, leaving_half, 1, 1)
        d_step = split_dot(x * q, sel, 1)
        through = split_dot(x_step * state_back, sel, 1)
        own = x_step.astype(BF).astype(F32) * p
        d_cumul = split_dot(dy * y - own, sel, 1) - through
        pair = split_dot(leaving * start, sel, 1)
        d_end = jnp.sum(through, axis=0, keepdims=True) + jnp.exp(end) * jnp.sum(
            pair, axis=0, keepdims=True
        )
        tri = jnp.where(order_mask(rows, reverse), 1.0, 0.0)
        d_log = dot(tri, d_cumul, 0, 0, precision=HI) + d_end
        d_step = d_step - rate * d_log
        d_raw = d_step / (1.0 + jnp.exp(-shifted))
        d_bias = d_bias + jnp.sum(d_raw, axis=0, keepdims=True)
        d_rate = d_rate + jnp.sum(d_log * logdec, axis=0, keepdims=True)
        results.append((d_x, d_b, d_c, d_raw))
    (fx, fb, fc, fs), (rx, rb, rc, rs) = results
    return mixed, fx, rx, jnp.stack([fb, fc, rb, rc]), jnp.stack([fs, rs]), d_bias, d_rate, d_skip


def chain_weights(totals, here, forward):
    count = totals.shape[0]
    k = jnp.arange(count)[:, None]
    j = jnp.arange(count)[None, :]
    if forward:
        between = (j > k) & (j < here)
        reached = jnp.arange(count) < here
    else:
        between = (j < k) & (j > here)
        reached = jnp.arange(count) > here
    logs = jnp.sum(jnp.where(between[:, :, None], totals[None], 0.0), axis=1)
    return jnp.where(reached[:, None], jnp.exp(logs), 0.0)


def neighbours(value, axis, steps):
    count = lax.axis_size(axis)
    first, last = (max(0, -steps), min(count, count - steps))
    return lax.ppermute(value, axis, [(source, source + steps) for source in range(first, last)])


def round_keep(value):
    rounded = lax.optimization_barrier(value.astype(BF))
    return rounded.astype(F32)


def conv_pair(padded, conv_weight, conv_bias):
    radius = conv_weight.shape[0] - 1
    length = padded.shape[0] - 2 * radius
    forward = conv_bias
    backward = conv_bias
    for k in range(radius + 1):
        forward = forward + conv_weight[k] * padded[radius - k : radius - k + length]
        backward = backward + conv_weight[k] * padded[radius + k : radius + k + length]
    return forward, backward


def local(token_ids, table, norm_gain, conv_weight, conv_bias, weight_b, weight_c, step_weight,
          step_bias, log_rate, skip_gain, out_grad):
    rows = token_ids.shape[0]
    width = table.shape[1]
    vocab = table.shape[0]
    heads = step_bias.shape[0]
    state = weight_b.shape[1]
    features = width * lax.axis_size("fsdp")
    all_heads = step_weight.shape[1]
    radius = conv_weight.shape[0] - 1
    here = lax.axis_index("ctx")

    table_sums = lax.psum(jnp.sum(table * table, axis=1), "fsdp")
    marked = token_ids + 1
    before = neighbours(marked[rows - radius :], "ctx", 1)
    after = neighbours(marked[:radius], "ctx", -1)
    marks = jnp.concatenate([before, marked, after])
    inverse = lax.rsqrt(table_sums / features + 1e-05)[:, None]
    unit_table = table * inverse
    normed_table = (unit_table * norm_gain).astype(BF)
    onehot_pad = (marks[:, None] == jnp.arange(1, vocab + 1)[None, :]).astype(BF)
    padded = dot(onehot_pad, normed_table)
    pre_f, pre_r = conv_pair(padded, conv_weight, conv_bias)
    xf = jax.nn.silu(pre_f).astype(BF)
    xr = jax.nn.silu(pre_r).astype(BF)
    joined_w = jnp.concatenate([weight_b, weight_c, step_weight], axis=1)
    both_x = jnp.concatenate([xf, xr], axis=0)
    parts = lax.psum(dot(both_x, joined_w), "fsdp")
    first_head = lax.axis_index("fsdp") * heads
    half = parts[:, : 2 * state].astype(BF)
    raws = lax.dynamic_slice_in_dim(parts[:, 2 * state :], first_head, heads, 1)
    bf, cf = half[:rows, :state], half[:rows, state:]
    br, cr = half[rows:, :state], half[rows:, state:]
    raw_f, raw_r = raws[:rows], raws[rows:]
    bias = step_bias[None]
    rate = log_rate[None]
    small = ((rows, heads), F32)
    one = ((1, heads), F32)
    states, cum_f, step_f, end_f, cum_r, step_r, end_r = whole_kernel(
        states_stage,
        [((4, state, width), BF), small, small, one, small, small, one],
        (raw_f, raw_r, bias, rate, xf, xr, bf, cf, br, cr, out_grad),
    )
    ends = lax.all_gather(jnp.concatenate([end_f, end_r]), "ctx")
    everything = lax.all_gather(states, "ctx")
    pairs = heads // 2

    def paired(value):
        return jnp.transpose(value.reshape(rows, pairs, 2), (1, 0, 2))

    cols = jnp.concatenate([paired(v) for v in (cum_f, cum_r, step_f, step_r)], axis=2)
    cut = jnp.transpose(cols[:, :, :4], (0, 2, 1))
    yf, yr, pf, pr, df, dr = intra_stage(cols, cut, xf, xr, out_grad, bf, cf, br, cr)
    weights = jnp.stack(
        [
            chain_weights(ends[:, 0], here, True),
            chain_weights(ends[:, 1], here, False),
            chain_weights(ends[:, 0], here, False),
            chain_weights(ends[:, 1], here, True),
        ],
        axis=1,
    )
    weights = jnp.repeat(weights, width // heads, axis=2)[:, :, None, :]
    chained = jnp.sum(everything.astype(F32) * weights, axis=0)
    mixer_out, d_fx, d_rx, d_bc, d_raw, d_bias, d_rate, d_skip = whole_kernel(
        joined_stage,
        [
            ((rows, width), BF),
            ((rows, width), F32),
            ((rows, width), F32),
            ((4, rows, state), BF),
            ((2, rows, heads), BF),
            one,
            one,
            one,
        ],
        (chained, yf, yr, pf, pr, df, dr, xf, xr, out_grad, bf, cf, br, cr, raw_f, raw_r,
         cum_f, cum_r, bias, rate, skip_gain[None]),
    )
    summed_bc = lax.psum(d_bc, "fsdp")
    every_raw = lax.all_gather(d_raw, "fsdp", axis=2, tiled=True)
    back = jnp.concatenate(
        [
            jnp.concatenate([summed_bc[0], summed_bc[1], every_raw[0]], axis=1),
            jnp.concatenate([summed_bc[2], summed_bc[3], every_raw[1]], axis=1),
        ],
        axis=0,
    )
    into = dot(back, joined_w, 1, 1)
    grad_w = lax.psum(dot(both_x, back, 0, 0), "ctx")

    def silu_back(pre, d_x):
        gate = jax.nn.sigmoid(pre)
        return d_x.astype(BF).astype(F32) * (gate * (1.0 + pre * (1.0 - gate)))

    pre_f, pre_r = conv_pair(padded, conv_weight, conv_bias)
    dp_f = silu_back(pre_f, d_fx + into[:rows])
    dp_r = silu_back(pre_r, d_rx + into[rows:])
    d_cb = jnp.sum(dp_f + dp_r, axis=0)
    d_cw = jnp.stack(
        [
            jnp.sum(
                dp_f * padded[radius - k : radius - k + rows]
                + dp_r * padded[radius + k : radius + k + rows],
                axis=0,
            )
            for k in range(radius + 1)
        ]
    )
    dp_f_after = neighbours(dp_f[:radius], "ctx", -1)
    dp_r_before = neighbours(dp_r[rows - radius :], "ctx", 1)
    long_f = jnp.concatenate([dp_f, dp_f_after], axis=0)
    long_r = jnp.concatenate([dp_r_before, dp_r], axis=0)
    center = 0.0
    for k in range(radius + 1):
        center = center + conv_weight[k] * (
            long_f[k : k + rows] + long_r[radius - k : radius - k + rows]
        )
    grad_normed = round_keep(center)
    onehot = (token_ids[:, None] == jnp.arange(vocab)[None, :]).astype(F32)
    scale = jnp.sum(onehot * inverse[:, 0], axis=1, keepdims=True)
    embedded = jnp.dot(onehot, table, precision=HI)
    grad_unit = grad_normed * norm_gain
    cross = lax.psum(jnp.sum(grad_unit * embedded, axis=1), "fsdp")[:, None]
    d_embedded = scale * grad_unit - embedded * (scale * scale * scale) * (cross / features)
    grad_embedded = d_embedded.astype(BF)
    d_table = jnp.dot(onehot.T, d_embedded, precision=HI)
    d_gain = jnp.sum(grad_normed * (embedded * scale), axis=0)
    wide = jnp.concatenate([d_table, d_gain[None], d_cw, d_cb[None]], axis=0)
    tiny = jnp.concatenate([d_bias, d_rate, d_skip], axis=0)
    wide, tiny = lax.psum((wide, tiny), "ctx")
    return (
        mixer_out,
        grad_embedded,
        wide[:vocab],
        wide[vocab],
        wide[vocab + 1 : vocab + 2 + radius],
        wide[vocab + 2 + radius],
        grad_w[:, :state],
        grad_w[:, state : 2 * state],
        grad_w[:, 2 * state :],
        tiny[0],
        tiny[1],
        tiny[2],
    )


def solution(mesh):
    return jax.shard_map(
        local,
        mesh=mesh,
        in_specs=(
            P("ctx"),
            P(None, "fsdp"),
            P("fsdp"),
            P(None, "fsdp"),
            P("fsdp"),
            P("fsdp", None),
            P("fsdp", None),
            P("fsdp", None),
            P("fsdp"),
            P("fsdp"),
            P("fsdp"),
            P("ctx", "fsdp"),
        ),
        out_specs=(
            P("ctx", "fsdp"),
            P("ctx", "fsdp"),
            P(None, "fsdp"),
            P("fsdp"),
            P(None, "fsdp"),
            P("fsdp"),
            P("fsdp", None),
            P("fsdp", None),
            P("fsdp", None),
            P("fsdp"),
            P("fsdp"),
            P("fsdp"),
        ),
        check_vma=False,
    )
```

profile of v0, /device:TPU:0, one launch (start us, length us, event | category | flops | bytes accessed | tf_op | source)
XLA Modules:
  0.0 375.0 jit_solution(14771577283156143688)
XLA Ops:
  8.0 4.8 %collective-permute-start = (s32[3]{0:T(128)S(1)}, s32[3]{0:T(128)S(1)}, u32[]{:S(2)}, u32[]{:S(2)}) collective-permute-start(s32[3]{0:T(128)S(1)} %get-tuple-element.140), channel_id=1, source_target_pairs={{0,1},{1,2},{2,3},{3,4},{4,5},{5,6},{6,7},{8,9},{9,10},{10,11},{11... | collective-permute-start | bytes 44 | tf_op jit(solution)/shard_map/ppermute | solution.py:244
  12.8 1.3 collective-permute-start.1
  15.1 6.3 %psum.49 = f32[16]{0:T(128)S(1)} all-reduce(f32[16]{0:T(128)S(1)} %multiply_reduce_fusion.1), channel_id=1, replica_groups=mesh['fsdp'=4,'ctx'=8] {'fsdp'}, use_global_device_ids=true, to_apply=%region_1.0 | all-reduce | flops 16 | bytes 128 | tf_op jit(solution)/shard_map/psum | solution.py:275
  22.3 1.1 copy.49
  23.5 1.2 fusion.25
  24.7 2.2 multiply_convert_fusion.1
  27.0 1.6 fusion.23
  28.7 36.7 %all-reduce.5.cloned.1.call-done = f32[512,320]{1,0:T(8,128)} async-done(((f32[512,320]{1,0:T(8,128)}), f32[512,320]{1,0:T(8,128)}) %all-reduce.5.cloned.1.call-update) | async-done | bytes 655376 | tf_op jit(solution)/shard_map/psum | solution.py:290
  65.3 1.2 convert.3
  68.2 6.1 %shard_map.211 = (bf16[4,128,1024]{2,1,0:T(8,128)(2,1)}, f32[256,16]{1,0:T(8,128)}, f32[256,16]{1,0:T(8,128)}, f32[1,16]{1,0:T(1,128)}, f32[256,16]{1,0:T(8,128)}, /*index=5*/f32[256,16]{1,0:T(8,128)}, f32[1,16]{1,0:T(1,128)}) custom-call(f32[256,16]{1,0:T(8,128)} %get-tuple-element.126.refs_0_.refs_14_, f32[256,16]{1,0:T(8,128)} %get-tuple-element.125.refs_1_.refs_15_, ...), custom_call_target="tpu_custom_call" | custom-call | tf_op jit(solution)/shard_map/pallas_call | solution.py:53
  75.2 20.9 %all-gather.2 = f32[8,2,16]{2,1,0:T(2,128)S(1)} all-gather(f32[1,2,16]{2,1,0:T(2,128)S(1)} %maximum_bitcast_fusion.1), channel_id=3, replica_groups=mesh['fsdp'=4,'ctx'=8] {'ctx'}, dimensions={0}, use_global_device_ids=true | all-gather | bytes 1152 | tf_op jit(solution)/shard_map/all_gather | solution.py:306
  98.9 1.3 copy.58.cols_ref
  100.8 10.3 %shard_map.212 = (f32[256,1024]{1,0:T(8,128)}, f32[256,1024]{1,0:T(8,128)}, f32[256,1024]{1,0:T(8,128)}, f32[256,1024]{1,0:T(8,128)}, f32[256,256]{1,0:T(8,128)}, /*index=5*/f32[256,256]{1,0:T(8,128)}) custom-call(f32[8,256,8]{2,1,0:T(8,128)} %copy.58.cols_ref, f32[8,4,256]{2,1,0:T(4,128)} %maximum_bitcast_fusion.cut_ref, bf16[256,1024]{1,0:T(8,128)(2,1)} %copy-done, ...), custom_call_target="tpu_custom_call" | custom-call | tf_op jit(solution)/shard_map/pallas_call | solution.py:145
  111.1 88.3 %all-gather.5.cloned.1.call-done = bf16[32,128,1024]{2,1,0:T(8,128)(2,1)} async-done(((bf16[4,128,1024]{2,1,0:T(8,128)(2,1)}), bf16[32,128,1024]{2,1,0:T(8,128)(2,1)}) %all-gather.5.cloned.1.call-update) | async-done | bytes 8388624 | tf_op jit(solution)/shard_map/all_gather | solution.py:307
  199.4 7.4 %fusion.refs_0_ = f32[4,128,1024]{2,1,0:T(8,128)} fusion(bf16[8,4,128,1024]{3,2,1,0:T(8,128)(2,1)} %bitcast.67, f32[8,4,1024]{2,1,0:T(4,128)S(1)} %mul.290), kind=kLoop, calls=%fused_computation.1 | loop fusion | flops 12058624 | bytes 10616832 | tf_op jit(solution)/shard_map/reduce_sum | solution.py:326
  206.9 11.8 %shard_map.213 = (bf16[256,1024]{1,0:T(8,128)(2,1)}, f32[256,1024]{1,0:T(8,128)}, f32[256,1024]{1,0:T(8,128)}, bf16[4,256,128]{2,1,0:T(8,128)(2,1)}, bf16[2,256,...) custom-call(f32[4,128,1024]{2,1,0:T(8,128)} %fusion.refs_0_, ...), custom_call_target="tpu_custom_call" | custom-call | tf_op jit(solution)/shard_map/pallas_call | solution.py:53
  219.7 5.5 %all_gather.19 = bf16[2,256,64]{1,0,2:T(2,128)(2,1)S(1)} all-gather(bf16[2,256,16]{1,0,2:T(2,128)(2,1)S(1)} %copy.59), channel_id=1, replica_groups=mesh['fsdp'=4,'ctx'=8] {'fsdp'}, dimensions={2}, use_global_device_ids=true | all-gather | bytes 81920 | tf_op jit(solution)/shard_map/all_gather | solution.py:343
  225.6 23.4 %all-reduce.7.cloned.1.call-done = bf16[4,256,128]{2,1,0:T(8,128)(2,1)} async-done(((bf16[4,256,128]{2,1,0:T(8,128)(2,1)}), bf16[4,256,128]{2,1,0:T(8,128)(2,1)}) %all-reduce.7.cloned.1.call-update) | async-done | bytes 262160 | tf_op jit(solution)/shard_map/psum | solution.py:342
  251.8 1.7 add_reduce_fusion
  253.6 3.4 collective-permute-start.3
  257.0 1.3 collective-permute-start.2
  258.3 1.6 fusion.22
  259.9 2.7 collective-permute-done.2
  264.3 5.8 %psum.52 = f32[256]{0:T(256)S(1)} all-reduce(f32[256]{0:T(256)S(1)} %get-tuple-element.96), channel_id=1, replica_groups=mesh['fsdp'=4,'ctx'=8] {'fsdp'}, use_global_device_ids=true, to_apply=%region_11.12 | all-reduce | flops 256 | bytes 2048 | tf_op jit(solution)/shard_map/psum | solution.py:386
  271.6 1.3 concatenate.50
  273.0 20.4 %psum.55 = f32[3,16]{1,0:T(4,128)S(1)} all-reduce(f32[3,16]{1,0:T(4,128)S(1)} %pad_maximum_fusion.10), channel_id=1, replica_groups=mesh['fsdp'=4,'ctx'=8] {'ctx'}, use_global_device_ids=true, to_apply=%region_20.21 | all-reduce | flops 48 | bytes 384 | tf_op jit(solution)/shard_map/psum | solution.py:393
  293.9 65.3 %all-reduce.9.cloned.1.call-done = (f32[22,1024]{1,0:T(8,128)}, f32[1024,320]{0,1:T(8,128)}) async-done(((f32[22,1024]{1,0:T(8,128)}, f32[1024,320]{0,1:T(8,128)}), (f32[22,1024]{1,0:T(8,128)}, f32[1024,320]{0,1:T(8,128)})) %all-reduce.9.cloned.1.call-update) | async-done | bytes 1400848 | tf_op jit(solution)/shard_map/psum | solution.py:393
  359.2 1.4 fusion.45
  360.7 1.4 slice.269
  362.0 1.5 slice.267
  363.5 1.7 slice.273
  365.2 1.3 fusion.42
  (103 shorter events, 18.6 us)
Async XLA Ops:
  7.2 17.5 %copy-start.12 = (f32[1024]{0:T(1024)S(1)}, f32[1024]{0:T(1024)}, u32[]{:S(2)}) copy-start(f32[1024]{0:T(1024)} %param.16) | copy-start | bytes 12292
  7.2 58.1 %all-reduce.5.cloned.1.call-start = ((), (), s32[]{:S(2)}) async-start(), calls=%async_computation | async-start | bytes 1572864 | tf_op jit(solution)/shard_map/psum | solution.py:290
  8.0 15.4 %collective-permute-start = (s32[3]{0:T(128)S(1)}, s32[3]{0:T(128)S(1)}, u32[]{:S(2)}, u32[]{:S(2)}) collective-permute-start(s32[3]{0:T(128)S(1)} %get-tuple-element.140), channel_id=1, source_target_pairs={{0,1},{1,2},{2,3},{3,4},{4,5},{5,6},{6,7},{8,9},{9,10},{10,11},{11... | collective-permute-start | bytes 44 | tf_op jit(solution)/shard_map/ppermute | solution.py:244
  12.8 10.6 %collective-permute-start.1 = (s32[3]{0:T(128)S(1)}, s32[3]{0:T(128)S(1)}, u32[]{:S(2)}, u32[]{:S(2)}) collective-permute-start(s32[3]{0:T(128)S(1)} %get-tuple-element.141), channel_id=1, source_target_pairs={{1,0},{2,1},{3,2},{4,3},{5,4},{6,5},{7,6},{9,8},{10,9},{11,10},{12... | collective-permute-start | bytes 44 | tf_op jit(solution)/shard_map/ppermute | solution.py:244
  24.7 2.3 copy-start.16
  24.7 2.2 copy-start.18
  27.0 1.6 copy-start
  27.0 1.6 copy-start.2
  28.6 170.8 %all-gather.5.cloned.1.call-start = ((), (), s32[]{:S(2)}) async-start(), calls=%async_computation.2 | async-start | bytes 9437184 | tf_op jit(solution)/shard_map/all_gather | solution.py:307
  65.3 2.0 slice-start
  68.2 6.2 %copy-start.11 = (s32[256]{0:T(256)S(1)}, s32[256]{0:T(256)}, u32[]{:S(2)}) copy-start(s32[256]{0:T(256)} %param.12) | copy-start | bytes 3076
  74.3 24.1 %copy-start.7 = (f32[256,16]{1,0:T(8,128)S(1)}, f32[256,16]{1,0:T(8,128)}, u32[]{:S(2)}) copy-start(f32[256,16]{1,0:T(8,128)} %get-tuple-element.36.refs_16_) | copy-start | bytes 49156
  74.3 24.2 %copy-start.8 = (f32[256,16]{1,0:T(8,128)S(1)}, f32[256,16]{1,0:T(8,128)}, u32[]{:S(2)}) copy-start(f32[256,16]{1,0:T(8,128)} %get-tuple-element.37.refs_17_) | copy-start | bytes 49156
  74.3 174.7 %all-reduce.7.cloned.1.call-start = ((), (), s32[]{:S(2)}) async-start(), calls=%async_computation.1 | async-start | bytes 524288 | tf_op jit(solution)/shard_map/psum | solution.py:342
  206.9 43.1 %copy-start.17 = (bf16[1024,128]{1,0:T(8,128)(2,1)S(1)}, bf16[1024,128]{1,0:T(8,128)(2,1)}, u32[]{:S(2)}) copy-start(bf16[1024,128]{1,0:T(8,128)(2,1)} %param.18) | copy-start | bytes 786436
  206.9 43.1 %copy-start.19 = (bf16[1024,128]{1,0:T(8,128)(2,1)S(1)}, bf16[1024,128]{1,0:T(8,128)(2,1)}, u32[]{:S(2)}) copy-start(bf16[1024,128]{1,0:T(8,128)(2,1)} %param.17) | copy-start | bytes 786436
  218.7 140.5 %all-reduce.9.cloned.1.call-start = ((), (), s32[]{:S(2)}) async-start(), calls=%async_computation.3 | async-start | bytes 2818048 | tf_op jit(solution)/shard_map/psum | solution.py:393
  250.0 1.2 copy-start.4
  250.0 1.5 copy-start.5
  250.0 1.8 copy-start.6
  251.8 6.4 %copy-start.1 = (bf16[256,1024]{1,0:T(8,128)(2,1)S(1)}, bf16[256,1024]{1,0:T(8,128)(2,1)}, u32[]{:S(2)}) copy-start(bf16[256,1024]{1,0:T(8,128)(2,1)} %copy-done) | copy-start | bytes 1572868
  251.8 6.4 %copy-start.3 = (bf16[256,1024]{1,0:T(8,128)(2,1)S(1)}, bf16[256,1024]{1,0:T(8,128)(2,1)}, u32[]{:S(2)}) copy-start(bf16[256,1024]{1,0:T(8,128)(2,1)} %copy-done.2) | copy-start | bytes 1572868
  253.6 6.4 %collective-permute-start.3 = (f32[3,1024]{1,0:T(4,128)S(1)}, f32[3,1024]{1,0:T(4,128)S(1)}, u32[]{:S(2)}, u32[]{:S(2)}) collective-permute-start(f32[3,1024]{1,0:T(4,128)S(1)} %slice.260), channel_id=1, source_target_pairs={{0,1},{1,2},{2,3},{3,4},{4,5},{5,6},{6,7},{8,9},{9,10},{10,11},{11... | collective-permute-start | bytes 36872 | tf_op jit(solution)/shard_map/ppermute | solution.py:244
  257.0 5.6 %collective-permute-start.2 = (f32[3,1024]{1,0:T(4,128)S(1)}, f32[3,1024]{1,0:T(4,128)S(1)}, u32[]{:S(2)}, u32[]{:S(2)}) collective-permute-start(f32[3,1024]{1,0:T(4,128)S(1)} %slice.257), channel_id=1, source_target_pairs={{1,0},{2,1},{3,2},{4,3},{5,4},{6,5},{7,6},{9,8},{10,9},{11,10},{12... | collective-permute-start | bytes 36872 | tf_op jit(solution)/shard_map/ppermute | solution.py:244
  259.9 3.5 copy-start.9
  259.9 3.5 copy-start.10
  271.2 1.8 copy-start.13
  271.2 1.8 copy-start.14
  271.2 1.8 copy-start.15
Sparse Core Ops, SparseCore 0:
  28.7 36.5 all-reduce.4
  74.4 124.9 all-gather.4
  218.8 30.1 all-reduce.6
  273.1 86.0 all-reduce.8
where the time goes:
time: 376 us; the launch traced here: 375 us
  waiting for transfers between devices  216 us (57%)
  blocking collectives  58.8 us (16%)
  Pallas kernels  28.2 us (8%)
  local copies, waits for them, and re-layouts  21.9 us (6%)
  other arithmetic  18 us (5%)
  between operations  14.2 us (4%)
  starting transfers between devices  10.9 us (3%)
  matrix products  6.52 us (2%)
    all_gather x1, waiting for transfers between devices, local(): everything = lax.all_gather(states, 'ctx')  88.3 us
    psum x1, waiting for transfers between devices, local(): wide, tiny = lax.psum((wide, tiny), 'ctx')  65.3 us
    psum x1, waiting for transfers between devices, local(): parts = lax.psum(dot(both_x, joined_w), 'fsdp')  36.7 us
    psum x1, waiting for transfers between devices, local(): summed_bc = lax.psum(d_bc, 'fsdp')  23.4 us
    all_gather x1, blocking collectives, local(): ends = lax.all_gather(jnp.concatenate([end_f, end_r]), 'ctx')  20.9 us
    psum x1, blocking collectives, local(): wide, tiny = lax.psum((wide, tiny), 'ctx')  20.4 us
    pallas_call x2, Pallas kernels, whole_kernel(): pl.pallas_call(body, out_shape=tuple((jax.ShapeDtypeStruct(s, d) for s, d...  17.9 us
    ppermute x4, starting transfers between devices, neighbours(): lax.ppermute(value, axis, [(source, source + steps) for source in range(f...  10.8 us
  transfers between devices with their start and end apart: 8, of which 5 were waited for; matrix products, arithmetic and copies ran while one was open for 3% of the time, Pallas kernels for 3%

commit v1 on v0

--- a/solution.py
+++ b/solution.py
@@ -75,16 +75,9 @@
         states.append(dot(b, xs, 0, 0))
         gy = (split_dot(jnp.exp(cumul), sel) * dy.astype(F32)).astype(BF)
         dstates.append(dot(c, gy, 0, 0))
-        cols += [cumul, step, end]
-    return (
-        jnp.stack(states + dstates),
-        cols[0],
-        cols[1],
-        cols[2],
-        cols[3],
-        cols[4],
-        cols[5],
-    )
+        wide_end = split_dot(jnp.broadcast_to(jnp.exp(end), (8, heads)), sel)
+        cols += [cumul, step, wide_end]
+    return (jnp.stack(states + dstates),) + tuple(cols)
 
 
 def intra_kernel(cols_ref, cut_ref, xf_ref, xr_ref, dy_ref, bf_ref, cf_ref, br_ref, cr_ref,
@@ -224,18 +217,238 @@
     return mixed, fx, rx, jnp.stack([fb, fc, rb, rc]), jnp.stack([fs, rs]), d_bias, d_rate, d_skip
 
 
-def chain_weights(totals, here, forward):
-    count = totals.shape[0]
-    k = jnp.arange(count)[:, None]
-    j = jnp.arange(count)[None, :]
-    if forward:
-        between = (j > k) & (j < here)
-        reached = jnp.arange(count) < here
-    else:
-        between = (j < k) & (j > here)
-        reached = jnp.arange(count) > here
-    logs = jnp.sum(jnp.where(between[:, :, None], totals[None], 0.0), axis=1)
-    return jnp.where(reached[:, None], jnp.exp(logs), 0.0)
+MESH = pl.DeviceIdType.MESH
+
+
+def greet_all(axis, count, here):
+    barrier = pltpu.get_barrier_semaphore()
+    for d in range(1, count):
+        pl.semaphore_signal(
+            barrier, inc=1, device_id={axis: lax.rem(here + d, count)}, device_id_type=MESH
+        )
+    pl.semaphore_wait(barrier, count - 1)
+
+
+def exchange(arrays, modes, axis, collective_id):
+    count = lax.axis_size(axis)
+    many = len(arrays)
+
+    def body(*refs):
+        ins, outs, bufs = refs[:many], refs[many : 2 * many], refs[2 * many : 3 * many]
+        send, recv = refs[3 * many :]
+        here = lax.axis_index(axis)
+        greet_all(axis, count, here)
+        copies = []
+        for d in range(1, count):
+            for k in range(many):
+                copy = pltpu.make_async_remote_copy(
+                    src_ref=ins[k],
+                    dst_ref=bufs[k].at[d - 1],
+                    send_sem=send.at[k, d - 1],
+                    recv_sem=recv.at[k, d - 1],
+                    device_id={axis: lax.rem(here + d, count)},
+                    device_id_type=MESH,
+                )
+                copy.start()
+                copies.append(copy)
+        for copy in copies:
+            copy.wait()
+        for k in range(many):
+            if modes[k] == "sum":
+                total = ins[k][...].astype(F32)
+                for d in range(1, count):
+                    total = total + bufs[k][d - 1].astype(F32)
+                outs[k][...] = total.astype(outs[k].dtype)
+            else:
+                outs[k][here] = ins[k][...]
+                for d in range(1, count):
+                    outs[k][lax.rem(here - d + count, count)] = bufs[k][d - 1]
+
+    shapes = [
+        jax.ShapeDtypeStruct(a.shape if m == "sum" else (count,) + a.shape, a.dtype)
+        for a, m in zip(arrays, modes)
+    ]
+    return pl.pallas_call(
+        body,
+        out_shape=tuple(shapes),
+        in_specs=[pl.BlockSpec(memory_space=pltpu.VMEM)] * many,
+        out_specs=tuple([pl.BlockSpec(memory_space=pltpu.VMEM)] * many),
+        scratch_shapes=[pltpu.VMEM((count - 1,) + a.shape, a.dtype) for a in arrays]
+        + [pltpu.SemaphoreType.DMA((many, count - 1)), pltpu.SemaphoreType.DMA((many, count - 1))],
+        compiler_params=pltpu.CompilerParams(
+            collective_id=collective_id, has_side_effects=True, vmem_limit_bytes=VMEM_LIMIT
+        ),
+    )(*arrays)
+
+
+def reduce_all(arrays, axis, collective_id):
+    count = lax.axis_size(axis)
+    many = len(arrays)
+    chunks = [a.shape[0] // count for a in arrays]
+
+    def body(*refs):
+        ins, outs = refs[:many], refs[many : 2 * many]
+        first, second = refs[2 * many : 3 * many], refs[3 * many : 4 * many]
+        mine = refs[4 * many : 5 * many]
+        send1, recv1, send2, recv2 = refs[5 * many :]
+        here = lax.axis_index(axis)
+
+        def rows(k, who):
+            return pl.ds(pl.multiple_of(who * chunks[k], chunks[k]), chunks[k])
+
+        greet_all(axis, count, here)
+        copies = {}
+        for d in range(1, count):
+            peer = lax.rem(here + d, count)
+            for k in range(many):
+                copies[k, d] = pltpu.make_async_remote_copy(
+                    src_ref=ins[k].at[rows(k, peer)],
+                    dst_ref=first[k].at[d - 1],
+                    send_sem=send1.at[k, d - 1],
+                    recv_sem=recv1.at[k, d - 1],
+                    device_id={axis: peer},
+                    device_id_type=MESH,
+                )
+                copies[k, d].start()
+        for k in range(many):
+            total = ins[k][rows(k, here)].astype(F32)
+            for d in range(1, count):
+                copies[k, d].wait()
+                total = total + first[k][d - 1].astype(F32)
+            mine[k][...] = total.astype(mine[k].dtype)
+            for d in range(1, count):
+                copies[k, d] = pltpu.make_async_remote_copy(
+                    src_ref=mine[k],
+                    dst_ref=second[k].at[d - 1],
+                    send_sem=send2.at[k, d - 1],
+                    recv_sem=recv2.at[k, d - 1],
+                    device_id={axis: lax.rem(here + d, count)},
+                    device_id_type=MESH,
+                )
+                copies[k, d].start()
+            outs[k][rows(k, here)] = mine[k][...].astype(F32)
+        for k in range(many):
+            for d in range(1, count):
+                copies[k, d].wait()
+                outs[k][rows(k, lax.rem(here - d + count, count))] = second[k][d - 1].astype(F32)
+
+    lanes = [a.shape[1] for a in arrays]
+    slots = [
+        pltpu.VMEM((count - 1, c, w), a.dtype) for a, c, w in zip(arrays, chunks, lanes)
+    ]
+    return pl.pallas_call(
+        body,
+        out_shape=tuple(jax.ShapeDtypeStruct(a.shape, F32) for a in arrays),
+        in_specs=[pl.BlockSpec(memory_space=pltpu.VMEM)] * many,
+        out_specs=tuple([pl.BlockSpec(memory_space=pltpu.VMEM)] * many),
+        scratch_shapes=slots
+        + slots
+        + [pltpu.VMEM((c, w), a.dtype) for a, c, w in zip(arrays, chunks, lanes)]
+        + [pltpu.SemaphoreType.DMA((many, count - 1))] * 4,
+        compiler_params=pltpu.CompilerParams(
+            collective_id=collective_id, has_side_effects=True, vmem_limit_bytes=VMEM_LIMIT
+        ),
+    )(*arrays)
+
+
+PIECE = 16
+
+
+def chain(states, decays, axis, collective_id):
+    count = lax.axis_size(axis)
+    kinds, depth, width = states.shape
+    pieces = depth // PIECE
+    routes = (((0, 0), (3, 1)), ((1, 1), (2, 0)))
+
+    def body(own, decay, out, inbox, outbox, send, recv):
+        here = lax.axis_index(axis)
+        following = lax.rem(here + 1, count)
+        previous = lax.rem(here - 1 + count, count)
+        barrier = pltpu.get_barrier_semaphore()
+        for who in (previous, following):
+            pl.semaphore_signal(barrier, inc=1, device_id={axis: who}, device_id_type=MESH)
+        pl.semaphore_wait(barrier, 2)
+
+        def copy_of(way, j):
+            return pltpu.make_async_remote_copy(
+                src_ref=outbox.at[way, j],
+                dst_ref=inbox.at[way, j],
+                send_sem=send.at[way, j],
+                recv_sem=recv.at[way, j],
+                device_id={axis: following if way == 0 else previous},
+                device_id_type=MESH,
+            )
+
+        def has_next(way):
+            return here < count - 1 if way == 0 else here > 0
+
+        def tick(t, carry):
+            for way in range(2):
+                rank = here if way == 0 else count - 1 - here
+                j = t - rank
+
+                @pl.when((j >= 0) & (j < pieces))
+                def _(way=way, rank=rank, j=j):
+                    @pl.when(rank > 0)
+                    def _():
+                        copy_of(way, j).wait_recv()
+
+                    @pl.when(rank == 0)
+                    def _():
+                        inbox[way, j] = jnp.zeros((2, PIECE, width), BF)
+
+                    for item, (kind, branch) in enumerate(routes[way]):
+                        entering = inbox[way, j, item]
+                        out[kind, j] = entering
+                        outbox[way, j, item] = (
+                            decay[branch : branch + 1, :] * entering.astype(F32)
+                            + own[kind, j].astype(F32)
+                        ).astype(BF)
+
+                    @pl.when(has_next(way))
+                    def _():
+                        copy_of(way, j).start()
+
+            return carry
+
+        lax.fori_loop(0, count + pieces - 1, tick, 0)
+
+        def finish(j, carry):
+            for way in range(2):
+
+                @pl.when(has_next(way))
+                def _(way=way):
+                    copy_of(way, j).wait_send()
+
+            return carry
+
+        lax.fori_loop(0, pieces, finish, 0)
+
+    shape = (kinds, pieces, PIECE, width)
+    box = pltpu.VMEM((2, pieces, 2, PIECE, width), BF)
+    result = pl.pallas_call(
+        body,
+        out_shape=jax.ShapeDtypeStruct(shape, BF),
+        in_specs=[pl.BlockSpec(memory_space=pltpu.VMEM)] * 2,
+        out_specs=pl.BlockSpec(memory_space=pltpu.VMEM),
+        scratch_shapes=[
+            box,
+            box,
+            pltpu.SemaphoreType.DMA((2, pieces)),
+            pltpu.SemaphoreType.DMA((2, pieces)),
+        ],
+        compiler_params=pltpu.CompilerParams(
+            collective_id=collective_id, has_side_effects=True, vmem_limit_bytes=VMEM_LIMIT
+        ),
+    )(states.reshape(shape), decays)
+    return result.reshape(states.shape)
+
+
+def as_rows(values, unit):
+    flat = jnp.concatenate([v.reshape(-1) for v in values])
+    size = flat.shape[0]
+    padded = -(-size // (128 * unit)) * (128 * unit)
+    return jnp.pad(flat, (0, padded - size)).reshape(-1, 128)
 
 
 def neighbours(value, axis, steps):
@@ -287,10 +500,11 @@
     xr = jax.nn.silu(pre_r).astype(BF)
     joined_w = jnp.concatenate([weight_b, weight_c, step_weight], axis=1)
     both_x = jnp.concatenate([xf, xr], axis=0)
-    parts = lax.psum(dot(both_x, joined_w), "fsdp")
+    parts = dot(both_x, joined_w[:, : 2 * state]).astype(BF)
+    raw_parts = dot(step_weight, both_x, 0, 1)
+    half, raw_sums = exchange((parts, raw_parts), ("sum", "sum"), "fsdp", 1)
     first_head = lax.axis_index("fsdp") * heads
-    half = parts[:, : 2 * state].astype(BF)
-    raws = lax.dynamic_slice_in_dim(parts[:, 2 * state :], first_head, heads, 1)
+    raws = lax.dynamic_slice_in_dim(raw_sums, first_head, heads, 0).T
     bf, cf = half[:rows, :state], half[:rows, state:]
     br, cr = half[rows:, :state], half[rows:, state:]
     raw_f, raw_r = raws[:rows], raws[rows:]
@@ -298,13 +512,14 @@
     rate = log_rate[None]
     small = ((rows, heads), F32)
     one = ((1, heads), F32)
+    ends = ((8, width), F32)
     states, cum_f, step_f, end_f, cum_r, step_r, end_r = whole_kernel(
         states_stage,
-        [((4, state, width), BF), small, small, one, small, small, one],
+        [((4, state, width), BF), small, small, ends, small, small, ends],
         (raw_f, raw_r, bias, rate, xf, xr, bf, cf, br, cr, out_grad),
     )
-    ends = lax.all_gather(jnp.concatenate([end_f, end_r]), "ctx")
-    everything = lax.all_gather(states, "ctx")
+    decays = jnp.concatenate([end_f[:1], end_r[:1]])
+    chained = chain(states, decays, "ctx", 2)
     pairs = heads // 2
 
     def paired(value):
@@ -313,17 +528,6 @@
     cols = jnp.concatenate([paired(v) for v in (cum_f, cum_r, step_f, step_r)], axis=2)
     cut = jnp.transpose(cols[:, :, :4], (0, 2, 1))
     yf, yr, pf, pr, df, dr = intra_stage(cols, cut, xf, xr, out_grad, bf, cf, br, cr)
-    weights = jnp.stack(
-        [
-            chain_weights(ends[:, 0], here, True),
-            chain_weights(ends[:, 1], here, False),
-            chain_weights(ends[:, 0], here, False),
-            chain_weights(ends[:, 1], here, True),
-        ],
-        axis=1,
-    )
-    weights = jnp.repeat(weights, width // heads, axis=2)[:, :, None, :]
-    chained = jnp.sum(everything.astype(F32) * weights, axis=0)
     mixer_out, d_fx, d_rx, d_bc, d_raw, d_bias, d_rate, d_skip = whole_kernel(
         joined_stage,
         [
@@ -339,8 +543,12 @@
         (chained, yf, yr, pf, pr, df, dr, xf, xr, out_grad, bf, cf, br, cr, raw_f, raw_r,
          cum_f, cum_r, bias, rate, skip_gain[None]),
     )
-    summed_bc = lax.psum(d_bc, "fsdp")
-    every_raw = lax.all_gather(d_raw, "fsdp", axis=2, tiled=True)
+    raw_rows = jnp.transpose(d_raw, (0, 2, 1)).reshape(2 * heads, rows)
+    raw_rows = jnp.pad(raw_rows, ((0, -2 * heads % PIECE), (0, 0)))
+    summed_bc, every = exchange((d_bc, raw_rows), ("sum", "gather"), "fsdp", 3)
+    every_raw = [
+        every[:, k * heads : (k + 1) * heads].reshape(all_heads, rows).T for k in range(2)
+    ]
     back = jnp.concatenate(
         [
             jnp.concatenate([summed_bc[0], summed_bc[1], every_raw[0]], axis=1),
@@ -349,7 +557,7 @@
         axis=0,
     )
     into = dot(back, joined_w, 1, 1)
-    grad_w = lax.psum(dot(both_x, back, 0, 0), "ctx")
+    grad_w = dot(both_x, back, 0, 0).astype(BF)
 
     def silu_back(pre, d_x):
         gate = jax.nn.sigmoid(pre)
@@ -388,22 +596,28 @@
     grad_embedded = d_embedded.astype(BF)
     d_table = jnp.dot(onehot.T, d_embedded, precision=HI)
     d_gain = jnp.sum(grad_normed * (embedded * scale), axis=0)
-    wide = jnp.concatenate([d_table, d_gain[None], d_cw, d_cb[None]], axis=0)
-    tiny = jnp.concatenate([d_bias, d_rate, d_skip], axis=0)
-    wide, tiny = lax.psum((wide, tiny), "ctx")
+    parts = (d_table, d_gain, d_cw, d_cb, d_bias, d_rate, d_skip)
+    shards = lax.axis_size("ctx")
+    weight_rows, rest_rows = reduce_all(
+        (as_rows((grad_w,), 16 * shards), as_rows(parts, 8 * shards)), "ctx", 4
+    )
+    grad_w = weight_rows.reshape(-1)[: grad_w.size].reshape(grad_w.shape)
+    rest = rest_rows.reshape(-1)
+    outs = []
+    for part, shape in zip(
+        parts,
+        (d_table.shape, (width,), conv_weight.shape, (width,), (heads,), (heads,), (heads,)),
+    ):
+        outs.append(rest[: part.size].reshape(shape))
+        rest = rest[part.size :]
     return (
         mixer_out,
         grad_embedded,
-        wide[:vocab],
-        wide[vocab],
-        wide[vocab + 1 : vocab + 2 + radius],
-        wide[vocab + 2 + radius],
+        *outs[:4],
         grad_w[:, :state],
         grad_w[:, state : 2 * state],
         grad_w[:, 2 * state :],
-        tiny[0],
-        tiny[1],
-        tiny[2],
+        *outs[4:],
     )
 
 

time: 376 us -> 236 us (0.63)
  waiting for transfers between devices: 216 us -> 0.01 us
  Pallas kernels: 28.2 us -> 164 us
  blocking collectives: 58.8 us -> 13.4 us
  between operations: 14.2 us -> 1.13 us
  other arithmetic: 18 us -> 9.98 us
  local copies, waits for them, and re-layouts: 21.9 us -> 27.4 us
    pallas_call x0 -> x4, Pallas kernels: none -> 136 us  [the longest x1 60.6 us: chain(): pl.pallas_call(body, out_shape=jax.ShapeDtypeStruct(shape, BF), in_specs=...]
    psum x3 -> x0, waiting for transfers between devices: 125 us -> none  [the longest x1 65.3 us: local(): wide, tiny = lax.psum((wide, tiny), 'ctx')]
    all_gather x1 -> x0, waiting for transfers between devices: 88.3 us -> none  [local(): everything = lax.all_gather(states, 'ctx')]
    all_gather x2 -> x0, blocking collectives: 26.4 us -> none  [the longest x1 20.9 us: local(): ends = lax.all_gather(jnp.concatenate([end_f, end_r]), 'ctx')]
    psum x1 -> x0, blocking collectives: 20.4 us -> none  [local(): wide, tiny = lax.psum((wide, tiny), 'ctx')]
    reduce_sum x2 -> x0, other arithmetic: 7.55 us -> none  [the longest x1 7.43 us: local(): chained = jnp.sum(everything.astype(F32) * weights, axis=0)]
    reshape x0 -> x6, local copies, waits for them, and re-layouts: none -> 3.91 us  [the longest x2 2.41 us: as_rows(): return jnp.pad(flat, (0, padded - size)).reshape(-1, 128)]
  transfers between devices with their start and end apart: 8 -> 4, of which waited for: 5 -> 0; matrix products, arithmetic and copies ran while one was open for 3% -> 3% of each run, Pallas kernels for 3% -> 0%
where the time goes in v1:
time: 236 us; the launch traced here: 235 us
  Pallas kernels  164 us (69%)
  local copies, waits for them, and re-layouts  27.4 us (12%)
  blocking collectives  13.4 us (6%)
  starting transfers between devices  12.2 us (5%)
  other arithmetic  9.98 us (4%)
  matrix products  7.16 us (3%)
    pallas_call x1, Pallas kernels, chain(): pl.pallas_call(body, out_shape=jax.ShapeDtypeStruct(shape, BF), in_specs=...  60.6 us
    pallas_call x1, Pallas kernels, reduce_all(): pl.pallas_call(body, out_shape=tuple((jax.ShapeDtypeStruct(a.shape, F32)...  40.6 us
    pallas_call x2, Pallas kernels, exchange(): pl.pallas_call(body, out_shape=tuple(shapes), in_specs=[pl.BlockSpec(memo...  35.2 us
    pallas_call x2, Pallas kernels, whole_kernel(): pl.pallas_call(body, out_shape=tuple((jax.ShapeDtypeStruct(s, d) for s, d...  17.4 us
    ppermute x4, starting transfers between devices, neighbours(): lax.ppermute(value, axis, [(source, source + steps) for source in range(f...  12.2 us
    pallas_call x1, Pallas kernels, intra_stage(): pl.pallas_call(intra_kernel, grid=(pairs,), in_specs=[pl.BlockSpec((1, ro...  10.2 us
    psum x1, blocking collectives, local(): cross = lax.psum(jnp.sum(grad_unit * embedded, axis=1), 'fsdp')[:, None]  7.04 us
    psum x1, blocking collectives, local(): table_sums = lax.psum(jnp.sum(table * table, axis=1), 'fsdp')  6.33 us
  transfers between devices with their start and end apart: 4, of which 0 were waited for; matrix products, arithmetic and copies ran while one was open for 3% of the time, Pallas kernels for 0%

profile of v1, /device:TPU:0, one launch (start us, length us, event | category | flops | bytes accessed | tf_op | source)
XLA Modules:
  0.0 235.2 jit_solution(11210844656641731647)
XLA Ops:
  1.4 4.8 %collective-permute-start = (s32[3]{0:T(128)S(1)}, s32[3]{0:T(128)S(1)}, u32[]{:S(2)}, u32[]{:S(2)}) collective-permute-start(s32[3]{0:T(128)S(1)} %get-tuple-element.128), channel_id=1, source_target_pairs={{0,1},{1,2},{2,3},{3,4},{4,5},{5,6},{6,7},{8,9},{9,10},{10,11},{11... | collective-permute-start | bytes 44 | tf_op jit(solution)/shard_map/ppermute | solution.py:457
  6.3 1.3 collective-permute-start.1
  8.5 6.3 %psum.14 = f32[16]{0:T(128)S(1)} all-reduce(f32[16]{0:T(128)S(1)} %multiply_reduce_fusion.1), channel_id=1, replica_groups=mesh['fsdp'=4,'ctx'=8] {'fsdp'}, use_global_device_ids=true, to_apply=%region_1.0 | all-reduce | flops 16 | bytes 128 | tf_op jit(solution)/shard_map/psum | solution.py:488
  15.8 1.1 copy.57
  17.7 1.2 fusion.30
  18.9 2.6 %multiply_convert_fusion.1 = (bf16[256,1024]{1,0:T(8,128)(2,1)S(1)}, f32[256,1024]{1,0:T(8,128)}, bf16[256,1024]{1,0:T(8,128)(2,1)S(1)}, f32[256,1024]{1,0:T(8,128)}) fusion(f32[262,1024]{1,0:T(8,128)S(1)} %fusion.30, f32[1024]{0:T(1024)S(1)} %bitcast.88, f32[1024]{0:T(1024)S(1)} %bitcast.90, f32[1024]{0:T(1024)S(1)} %bitcast.86, f32[1024]{0:T(1024)S(1)} %bitcast.84, ...), kind=kLoop, calls=%fused_computation.45 | loop fusion | flops 6291456 | bytes 10506240 | tf_op jit(solution)/shard_map/convert_element_type | solution.py:499
  21.5 1.1 convolution_bitcast_fusion.refs_1_
  22.9 1.1 convolution_convert_fusion.1.refs_0_
  24.0 20.4 %shard_map.211 = (bf16[512,256]{1,0:T(8,128)(2,1)}, f32[64,512]{1,0:T(8,128)}) custom-call(bf16[512,256]{1,0:T(8,128)(2,1)} %convolution_convert_fusion.1.refs_0_, f32[64,512]{1,0:T(8,128)} %convolution_bitcast_fusion.refs_1_), custom_call_target="tpu_custom_call" | custom-call | tf_op jit(solution)/shard_map/pallas_call | solution.py:271
  44.5 1.1 copy.48
  47.2 6.0 %shard_map.212 = (bf16[4,128,1024]{2,1,0:T(8,128)(2,1)}, f32[256,16]{1,0:T(8,128)}, f32[256,16]{1,0:T(8,128)}, f32[8,1024]{1,0:T(8,128)}, f32[256,16]{1,0:T(8,12...) custom-call(f32[256,16]{1,0:T(8,128)} %get-tuple-element.116.refs_0_.refs_14_, f32[256,16]{1,0:T(8,128)} %get-tuple-element.115.refs_1_.refs_15_, ...), custom_call_target="tpu_custom_call" | custom-call | tf_op jit(solution)/shard_map/pallas_call | solution.py:53
  53.1 1.0 copy.49
  54.1 1.0 copy.50
  55.1 1.0 copy.51
  56.1 1.0 copy.52
  57.8 1.3 copy.53.cols_ref
  60.6 10.2 %shard_map.214 = (f32[256,1024]{1,0:T(8,128)}, f32[256,1024]{1,0:T(8,128)}, f32[256,1024]{1,0:T(8,128)}, f32[256,1024]{1,0:T(8,128)}, f32[256,256]{1,0:T(8,128)}, /*index=5*/f32[256,256]{1,0:T(8,128)}) custom-call(f32[8,256,8]{2,1,0:T(8,128)} %copy.53.cols_ref, f32[8,4,256]{2,1,0:T(4,128)} %maximum_bitcast_fusion.cut_ref, bf16[256,1024]{1,0:T(8,128)(2,1)} %copy-done, ...), custom_call_target="tpu_custom_call" | custom-call | tf_op jit(solution)/shard_map/pallas_call | solution.py:138
  71.5 60.6 %shard_map.213 = bf16[4,8,16,1024]{3,2,1,0:T(8,128)(2,1)} custom-call(bf16[4,8,16,1024]{3,2,1,0:T(8,128)(2,1)} %bitcast.67, f32[2,1024]{1,0:T(2,128)} %pad_maximum_fusion.7.decay), custom_call_target="tpu_custom_call" | custom-call | tf_op jit(solution)/shard_map/pallas_call | solution.py:429
  132.1 11.4 %shard_map.215 = (bf16[256,1024]{1,0:T(8,128)(2,1)}, f32[256,1024]{1,0:T(8,128)}, f32[256,1024]{1,0:T(8,128)}, bf16[4,256,128]{2,1,0:T(8,128)(2,1)}, bf16[2,256,...) custom-call(bf16[4,128,1024]{2,1,0:T(8,128)(2,1)} %bitcast.66, ...), custom_call_target="tpu_custom_call" | custom-call | tf_op jit(solution)/shard_map/pallas_call | solution.py:53
  143.5 1.6 copy.54
  145.1 14.7 %shard_map.216 = (bf16[4,256,128]{2,1,0:T(8,128)(2,1)}, bf16[4,32,256]{2,1,0:T(8,128)(2,1)}) custom-call(bf16[4,256,128]{2,1,0:T(8,128)(2,1)} %get-tuple-element.56.refs_0_, bf16[32,256]{1,0:T(8,128)(2,1)} %bitcast.76), custom_call_target="tpu_custom_call" | custom-call | tf_op jit(solution)/shard_map/pallas_call | solution.py:271
  161.8 1.4 convolution_convert_fusion
  165.4 1.7 multiply_reduce_fusion
  167.1 1.3 collective-permute-start.2
  168.5 4.8 %collective-permute-start.3 = (f32[3,1024]{1,0:T(4,128)S(1)}, f32[3,1024]{1,0:T(4,128)S(1)}, u32[]{:S(2)}, u32[]{:S(2)}) collective-permute-start(f32[3,1024]{1,0:T(4,128)S(1)} %slice.274), channel_id=1, source_target_pairs={{0,1},{1,2},{2,3},{3,4},{4,5},{5,6},{6,7},{8,9},{9,10},{10,11},{11... | collective-permute-start | bytes 36872 | tf_op jit(solution)/shard_map/ppermute | solution.py:457
  173.3 1.4 copy.58
  174.7 1.8 reshape.119.refs_0_
  178.3 7.0 %psum.15 = f32[256]{0:T(256)S(1)} all-reduce(f32[256]{0:T(256)S(1)} %get-tuple-element.96), channel_id=1, replica_groups=mesh['fsdp'=4,'ctx'=8] {'fsdp'}, use_global_device_ids=true, to_apply=%region_4.5 | all-reduce | flops 256 | bytes 2048 | tf_op jit(solution)/shard_map/psum | solution.py:594
  186.8 40.6 %shard_map.217 = (f32[2560,128]{1,0:T(8,128)}, f32[192,128]{1,0:T(8,128)}) custom-call(bf16[2560,128]{1,0:T(8,128)(2,1)} %reshape.119.refs_0_, f32[192,128]{1,0:T(8,128)} %pad_bitcast_fusion.refs_1_), custom_call_target="tpu_custom_call" | custom-call | tf_op jit(solution)/shard_map/pallas_call | solution.py:339
  227.5 1.8 reshape_reshape.3
  229.3 1.0 fusion.45
  231.4 1.1 fusion.44
  (97 shorter events, 19.4 us)
Async XLA Ops:
  0.6 18.3 %copy-start.16 = (f32[1024]{0:T(1024)S(1)}, f32[1024]{0:T(1024)}, u32[]{:S(2)}) copy-start(f32[1024]{0:T(1024)} %param.16) | copy-start | bytes 12292
  1.4 16.2 %collective-permute-start = (s32[3]{0:T(128)S(1)}, s32[3]{0:T(128)S(1)}, u32[]{:S(2)}, u32[]{:S(2)}) collective-permute-start(s32[3]{0:T(128)S(1)} %get-tuple-element.128), channel_id=1, source_target_pairs={{0,1},{1,2},{2,3},{3,4},{4,5},{5,6},{6,7},{8,9},{9,10},{10,11},{11... | collective-permute-start | bytes 44 | tf_op jit(solution)/shard_map/ppermute | solution.py:457
  6.3 11.4 %collective-permute-start.1 = (s32[3]{0:T(128)S(1)}, s32[3]{0:T(128)S(1)}, u32[]{:S(2)}, u32[]{:S(2)}) collective-permute-start(s32[3]{0:T(128)S(1)} %get-tuple-element.129), channel_id=1, source_target_pairs={{1,0},{2,1},{3,2},{4,3},{5,4},{6,5},{7,6},{9,8},{10,9},{11,10},{12... | collective-permute-start | bytes 44 | tf_op jit(solution)/shard_map/ppermute | solution.py:457
  18.9 2.6 %copy-start.13 = (bf16[1024,64]{0,1:T(8,128)(2,1)S(1)}, bf16[1024,64]{0,1:T(8,128)(2,1)}, u32[]{:S(2)}) copy-start(bf16[1024,64]{0,1:T(8,128)(2,1)} %param.19) | copy-start | bytes 393220
  21.5 2.5 %copy-start = (bf16[256,1024]{1,0:T(8,128)(2,1)}, bf16[256,1024]{1,0:T(8,128)(2,1)S(1)}, u32[]{:S(2)}) copy-start(bf16[256,1024]{1,0:T(8,128)(2,1)S(1)} %get-tuple-element.99.refs_4_.xf_ref.refs_7_) | copy-start | bytes 1572868
  21.5 2.5 %copy-start.2 = (bf16[256,1024]{1,0:T(8,128)(2,1)}, bf16[256,1024]{1,0:T(8,128)(2,1)S(1)}, u32[]{:S(2)}) copy-start(bf16[256,1024]{1,0:T(8,128)(2,1)S(1)} %get-tuple-element.105.refs_5_.xr_ref.refs_8_) | copy-start | bytes 1572868
  21.5 1.1 copy-start.21
  21.5 1.4 copy-start.22
  44.5 1.9 copy-start.11
  132.0 29.8 %copy-start.1 = (bf16[256,1024]{1,0:T(8,128)(2,1)S(1)}, bf16[256,1024]{1,0:T(8,128)(2,1)}, u32[]{:S(2)}) copy-start(bf16[256,1024]{1,0:T(8,128)(2,1)} %copy-done) | copy-start | bytes 1572868
  132.0 29.8 %copy-start.3 = (bf16[256,1024]{1,0:T(8,128)(2,1)S(1)}, bf16[256,1024]{1,0:T(8,128)(2,1)}, u32[]{:S(2)}) copy-start(bf16[256,1024]{1,0:T(8,128)(2,1)} %copy-done.2) | copy-start | bytes 1572868
  163.2 1.2 copy-start.5
  163.2 1.5 copy-start.6
  163.2 1.9 copy-start.9
  163.3 2.2 copy-start.10
  167.1 9.4 %collective-permute-start.2 = (f32[3,1024]{1,0:T(4,128)S(1)}, f32[3,1024]{1,0:T(4,128)S(1)}, u32[]{:S(2)}, u32[]{:S(2)}) collective-permute-start(f32[3,1024]{1,0:T(4,128)S(1)} %slice.271), channel_id=1, source_target_pairs={{1,0},{2,1},{3,2},{4,3},{5,4},{6,5},{7,6},{9,8},{10,9},{11,10},{12... | collective-permute-start | bytes 36872 | tf_op jit(solution)/shard_map/ppermute | solution.py:457
  168.5 8.0 %collective-permute-start.3 = (f32[3,1024]{1,0:T(4,128)S(1)}, f32[3,1024]{1,0:T(4,128)S(1)}, u32[]{:S(2)}, u32[]{:S(2)}) collective-permute-start(f32[3,1024]{1,0:T(4,128)S(1)} %slice.274), channel_id=1, source_target_pairs={{0,1},{1,2},{2,3},{3,4},{4,5},{5,6},{6,7},{8,9},{9,10},{10,11},{11... | collective-permute-start | bytes 36872 | tf_op jit(solution)/shard_map/ppermute | solution.py:457
  176.5 0.9 copy-start.12
  176.5 0.9 copy-start.15
  176.5 0.9 copy-start.17
  177.4 8.7 %copy-start.7 = (bf16[256,1024]{1,0:T(8,128)(2,1)}, bf16[256,1024]{1,0:T(8,128)(2,1)S(1)}, u32[]{:S(2)}) copy-start(bf16[256,1024]{1,0:T(8,128)(2,1)S(1)} %fusion.10) | copy-start | bytes 1572868
  177.4 8.7 %copy-start.18 = (f32[1,16]{1,0:T(1,128)S(1)}, f32[1,16]{1,0:T(1,128)}, u32[]{:S(2)}) copy-start(f32[1,16]{1,0:T(1,128)} %get-tuple-element.61) | copy-start | bytes 196
  177.4 8.7 %copy-start.19 = (f32[1,16]{1,0:T(1,128)S(1)}, f32[1,16]{1,0:T(1,128)}, u32[]{:S(2)}) copy-start(f32[1,16]{1,0:T(1,128)} %get-tuple-element.62) | copy-start | bytes 196
  177.4 8.7 %copy-start.20 = (f32[1,16]{1,0:T(1,128)S(1)}, f32[1,16]{1,0:T(1,128)}, u32[]{:S(2)}) copy-start(f32[1,16]{1,0:T(1,128)} %get-tuple-element.63) | copy-start | bytes 196
  229.3 1.5 copy-start.4
  229.3 1.5 copy-start.14
  229.3 2.1 copy-start.8
  230.8 1.7 slice-start

commit v2 on v1

--- a/solution.py
+++ b/solution.py
@@ -242,7 +242,7 @@
         for d in range(1, count):
             for k in range(many):
                 copy = pltpu.make_async_remote_copy(
-                    src_ref=ins[k],
+                    src_ref=ins[k].at[lax.rem(here + d, count)] if modes[k] == "scatter" else ins[k],
                     dst_ref=bufs[k].at[d - 1],
                     send_sem=send.at[k, d - 1],
                     recv_sem=recv.at[k, d - 1],
@@ -254,8 +254,9 @@
         for copy in copies:
             copy.wait()
         for k in range(many):
-            if modes[k] == "sum":
-                total = ins[k][...].astype(F32)
+            if modes[k] != "gather":
+                own = ins[k][here] if modes[k] == "scatter" else ins[k][...]
+                total = own.astype(F32)
                 for d in range(1, count):
                     total = total + bufs[k][d - 1].astype(F32)
                 outs[k][...] = total.astype(outs[k].dtype)
@@ -264,16 +265,17 @@
                 for d in range(1, count):
                     outs[k][lax.rem(here - d + count, count)] = bufs[k][d - 1]
 
+    blocks = [a.shape[1:] if m == "scatter" else a.shape for a, m in zip(arrays, modes)]
     shapes = [
-        jax.ShapeDtypeStruct(a.shape if m == "sum" else (count,) + a.shape, a.dtype)
-        for a, m in zip(arrays, modes)
+        jax.ShapeDtypeStruct((count,) + a.shape if m == "gather" else blocks[i], a.dtype)
+        for i, (a, m) in enumerate(zip(arrays, modes))
     ]
     return pl.pallas_call(
         body,
         out_shape=tuple(shapes),
         in_specs=[pl.BlockSpec(memory_space=pltpu.VMEM)] * many,
         out_specs=tuple([pl.BlockSpec(memory_space=pltpu.VMEM)] * many),
-        scratch_shapes=[pltpu.VMEM((count - 1,) + a.shape, a.dtype) for a in arrays]
+        scratch_shapes=[pltpu.VMEM((count - 1,) + b, a.dtype) for a, b in zip(arrays, blocks)]
         + [pltpu.SemaphoreType.DMA((many, count - 1)), pltpu.SemaphoreType.DMA((many, count - 1))],
         compiler_params=pltpu.CompilerParams(
             collective_id=collective_id, has_side_effects=True, vmem_limit_bytes=VMEM_LIMIT
@@ -502,9 +504,9 @@
     both_x = jnp.concatenate([xf, xr], axis=0)
     parts = dot(both_x, joined_w[:, : 2 * state]).astype(BF)
     raw_parts = dot(step_weight, both_x, 0, 1)
-    half, raw_sums = exchange((parts, raw_parts), ("sum", "sum"), "fsdp", 1)
-    first_head = lax.axis_index("fsdp") * heads
-    raws = lax.dynamic_slice_in_dim(raw_sums, first_head, heads, 0).T
+    raw_parts = raw_parts.reshape(-1, heads, 2 * rows)
+    half, raw_sums = exchange((parts, raw_parts), ("sum", "scatter"), "fsdp", 1)
+    raws = raw_sums.T
     bf, cf = half[:rows, :state], half[:rows, state:]
     br, cr = half[rows:, :state], half[rows:, state:]
     raw_f, raw_r = raws[:rows], raws[rows:]

time: 236 us -> 233 us (0.987)
  Pallas kernels: 164 us -> 160 us
    pallas_call x2, Pallas kernels: 35.2 us -> 30.9 us  [exchange(): pl.pallas_call(body, out_shape=tuple(shapes), in_specs=[pl.BlockSpec(memo...]
where the time goes in v2:
time: 233 us; the launch traced here: 231 us
  Pallas kernels  160 us (69%)
  local copies, waits for them, and re-layouts  28 us (12%)
  blocking collectives  13.4 us (6%)
  starting transfers between devices  12.2 us (5%)
  other arithmetic  9.97 us (4%)
  matrix products  7.16 us (3%)
    pallas_call x1, Pallas kernels, chain(): pl.pallas_call(body, out_shape=jax.ShapeDtypeStruct(shape, BF), in_specs=...  60.6 us
    pallas_call x1, Pallas kernels, reduce_all(): pl.pallas_call(body, out_shape=tuple((jax.ShapeDtypeStruct(a.shape, F32)...  40.7 us
    pallas_call x2, Pallas kernels, exchange(): pl.pallas_call(body, out_shape=tuple(shapes), in_specs=[pl.BlockSpec(memo...  30.9 us
    pallas_call x2, Pallas kernels, whole_kernel(): pl.pallas_call(body, out_shape=tuple((jax.ShapeDtypeStruct(s, d) for s, d...  17.4 us
    ppermute x4, starting transfers between devices, neighbours(): lax.ppermute(value, axis, [(source, source + steps) for source in range(f...  12.2 us
    pallas_call x1, Pallas kernels, intra_stage(): pl.pallas_call(intra_kernel, grid=(pairs,), in_specs=[pl.BlockSpec((1, ro...  10.2 us
    psum x1, blocking collectives, local(): cross = lax.psum(jnp.sum(grad_unit * embedded, axis=1), 'fsdp')[:, None]  7.04 us
    psum x1, blocking collectives, local(): table_sums = lax.psum(jnp.sum(table * table, axis=1), 'fsdp')  6.33 us
  transfers between devices with their start and end apart: 4, of which 0 were waited for; matrix products, arithmetic and copies ran while one was open for 3% of the time, Pallas kernels for 0%

profile of v2, /device:TPU:0, one launch (start us, length us, event | category | flops | bytes accessed | tf_op | source)
XLA Modules:
  0.0 231.5 jit_solution(5560244462858299264)
XLA Ops:
  1.4 4.8 %collective-permute-start = (s32[3]{0:T(128)S(1)}, s32[3]{0:T(128)S(1)}, u32[]{:S(2)}, u32[]{:S(2)}) collective-permute-start(s32[3]{0:T(128)S(1)} %get-tuple-element.128), channel_id=1, source_target_pairs={{0,1},{1,2},{2,3},{3,4},{4,5},{5,6},{6,7},{8,9},{9,10},{10,11},{11... | collective-permute-start | bytes 44 | tf_op jit(solution)/shard_map/ppermute | solution.py:459
  6.3 1.3 collective-permute-start.1
  8.5 6.3 %psum.14 = f32[16]{0:T(128)S(1)} all-reduce(f32[16]{0:T(128)S(1)} %multiply_reduce_fusion.1), channel_id=1, replica_groups=mesh['fsdp'=4,'ctx'=8] {'fsdp'}, use_global_device_ids=true, to_apply=%region_1.0 | all-reduce | flops 16 | bytes 128 | tf_op jit(solution)/shard_map/psum | solution.py:490
  15.8 1.1 copy.57
  17.7 1.2 fusion.31
  18.9 2.6 %multiply_convert_fusion.1 = (bf16[256,1024]{1,0:T(8,128)(2,1)S(1)}, f32[256,1024]{1,0:T(8,128)}, bf16[256,1024]{1,0:T(8,128)(2,1)S(1)}, f32[256,1024]{1,0:T(8,128)}) fusion(f32[262,1024]{1,0:T(8,128)S(1)} %fusion.31, f32[1024]{0:T(1024)S(1)} %bitcast.90, f32[1024]{0:T(1024)S(1)} %bitcast.92, f32[1024]{0:T(1024)S(1)} %bitcast.88, f32[1024]{0:T(1024)S(1)} %bitcast.86, ...), kind=kLoop, calls=%fused_computation.44 | loop fusion | flops 6291456 | bytes 10506240 | tf_op jit(solution)/shard_map/convert_element_type | solution.py:501
  21.5 1.1 fusion.30
  22.9 1.1 convolution_convert_fusion.1.refs_0_
  24.0 16.2 %shard_map.211 = (bf16[512,256]{1,0:T(8,128)(2,1)}, f32[16,512]{1,0:T(8,128)}) custom-call(bf16[512,256]{1,0:T(8,128)(2,1)} %convolution_convert_fusion.1.refs_0_, f32[4,16,512]{2,1,0:T(8,128)} %bitcast.74), custom_call_target="tpu_custom_call" | custom-call | tf_op jit(solution)/shard_map/pallas_call | solution.py:273
  40.2 1.6 fusion.47
  43.4 6.0 %shard_map.212 = (bf16[4,128,1024]{2,1,0:T(8,128)(2,1)}, f32[256,16]{1,0:T(8,128)}, f32[256,16]{1,0:T(8,128)}, f32[8,1024]{1,0:T(8,128)}, f32[256,16]{1,0:T(8,12...) custom-call(f32[256,16]{1,0:T(8,128)} %get-tuple-element.116.refs_0_.refs_14_, f32[256,16]{1,0:T(8,128)} %get-tuple-element.115.refs_1_.refs_15_, ...), custom_call_target="tpu_custom_call" | custom-call | tf_op jit(solution)/shard_map/pallas_call | solution.py:53
  49.4 1.0 copy.49
  50.4 1.0 copy.50
  51.4 1.0 copy.51
  52.4 1.0 copy.52
  54.1 1.3 copy.53.cols_ref
  56.9 10.2 %shard_map.214 = (f32[256,1024]{1,0:T(8,128)}, f32[256,1024]{1,0:T(8,128)}, f32[256,1024]{1,0:T(8,128)}, f32[256,1024]{1,0:T(8,128)}, f32[256,256]{1,0:T(8,128)}, /*index=5*/f32[256,256]{1,0:T(8,128)}) custom-call(f32[8,256,8]{2,1,0:T(8,128)} %copy.53.cols_ref, f32[8,4,256]{2,1,0:T(4,128)} %maximum_bitcast_fusion.cut_ref, bf16[256,1024]{1,0:T(8,128)(2,1)} %copy-done, ...), custom_call_target="tpu_custom_call" | custom-call | tf_op jit(solution)/shard_map/pallas_call | solution.py:138
  67.7 60.6 %shard_map.213 = bf16[4,8,16,1024]{3,2,1,0:T(8,128)(2,1)} custom-call(bf16[4,8,16,1024]{3,2,1,0:T(8,128)(2,1)} %bitcast.67, f32[2,1024]{1,0:T(2,128)} %pad_maximum_fusion.7.decay), custom_call_target="tpu_custom_call" | custom-call | tf_op jit(solution)/shard_map/pallas_call | solution.py:431
  128.3 11.4 %shard_map.215 = (bf16[256,1024]{1,0:T(8,128)(2,1)}, f32[256,1024]{1,0:T(8,128)}, f32[256,1024]{1,0:T(8,128)}, bf16[4,256,128]{2,1,0:T(8,128)(2,1)}, bf16[2,256,...) custom-call(bf16[4,128,1024]{2,1,0:T(8,128)(2,1)} %bitcast.66, ...), custom_call_target="tpu_custom_call" | custom-call | tf_op jit(solution)/shard_map/pallas_call | solution.py:53
  139.8 1.6 copy.54
  141.3 14.7 %shard_map.216 = (bf16[4,256,128]{2,1,0:T(8,128)(2,1)}, bf16[4,32,256]{2,1,0:T(8,128)(2,1)}) custom-call(bf16[4,256,128]{2,1,0:T(8,128)(2,1)} %get-tuple-element.56.refs_0_, bf16[32,256]{1,0:T(8,128)(2,1)} %bitcast.78), custom_call_target="tpu_custom_call" | custom-call | tf_op jit(solution)/shard_map/pallas_call | solution.py:273
  158.1 1.4 convolution_convert_fusion
  161.7 1.7 multiply_reduce_fusion
  163.4 1.3 collective-permute-start.2
  164.7 4.8 %collective-permute-start.3 = (f32[3,1024]{1,0:T(4,128)S(1)}, f32[3,1024]{1,0:T(4,128)S(1)}, u32[]{:S(2)}, u32[]{:S(2)}) collective-permute-start(f32[3,1024]{1,0:T(4,128)S(1)} %slice.274), channel_id=1, source_target_pairs={{0,1},{1,2},{2,3},{3,4},{4,5},{5,6},{6,7},{8,9},{9,10},{10,11},{11... | collective-permute-start | bytes 36872 | tf_op jit(solution)/shard_map/ppermute | solution.py:459
  169.5 1.4 copy.58
  171.0 1.7 reshape.123.refs_0_
  174.5 7.0 %psum.15 = f32[256]{0:T(256)S(1)} all-reduce(f32[256]{0:T(256)S(1)} %get-tuple-element.96), channel_id=1, replica_groups=mesh['fsdp'=4,'ctx'=8] {'fsdp'}, use_global_device_ids=true, to_apply=%region_4.5 | all-reduce | flops 256 | bytes 2048 | tf_op jit(solution)/shard_map/psum | solution.py:596
  183.1 40.7 %shard_map.217 = (f32[2560,128]{1,0:T(8,128)}, f32[192,128]{1,0:T(8,128)}) custom-call(bf16[2560,128]{1,0:T(8,128)(2,1)} %reshape.123.refs_0_, f32[192,128]{1,0:T(8,128)} %pad_bitcast_fusion.refs_1_), custom_call_target="tpu_custom_call" | custom-call | tf_op jit(solution)/shard_map/pallas_call | solution.py:341
  223.7 1.8 reshape_reshape.3
  225.6 1.0 fusion.46
  227.7 1.1 fusion.45
  (94 shorter events, 19.4 us)
Async XLA Ops:
  0.6 18.2 %copy-start.15 = (f32[1024]{0:T(1024)S(1)}, f32[1024]{0:T(1024)}, u32[]{:S(2)}) copy-start(f32[1024]{0:T(1024)} %param.16) | copy-start | bytes 12292
  1.4 16.2 %collective-permute-start = (s32[3]{0:T(128)S(1)}, s32[3]{0:T(128)S(1)}, u32[]{:S(2)}, u32[]{:S(2)}) collective-permute-start(s32[3]{0:T(128)S(1)} %get-tuple-element.128), channel_id=1, source_target_pairs={{0,1},{1,2},{2,3},{3,4},{4,5},{5,6},{6,7},{8,9},{9,10},{10,11},{11... | collective-permute-start | bytes 44 | tf_op jit(solution)/shard_map/ppermute | solution.py:459
  6.3 11.4 %collective-permute-start.1 = (s32[3]{0:T(128)S(1)}, s32[3]{0:T(128)S(1)}, u32[]{:S(2)}, u32[]{:S(2)}) collective-permute-start(s32[3]{0:T(128)S(1)} %get-tuple-element.129), channel_id=1, source_target_pairs={{1,0},{2,1},{3,2},{4,3},{5,4},{6,5},{7,6},{9,8},{10,9},{11,10},{12... | collective-permute-start | bytes 44 | tf_op jit(solution)/shard_map/ppermute | solution.py:459
  18.9 2.6 %copy-start.12 = (bf16[1024,64]{0,1:T(8,128)(2,1)S(1)}, bf16[1024,64]{0,1:T(8,128)(2,1)}, u32[]{:S(2)}) copy-start(bf16[1024,64]{0,1:T(8,128)(2,1)} %param.19) | copy-start | bytes 393220
  21.5 2.5 %copy-start = (bf16[256,1024]{1,0:T(8,128)(2,1)}, bf16[256,1024]{1,0:T(8,128)(2,1)S(1)}, u32[]{:S(2)}) copy-start(bf16[256,1024]{1,0:T(8,128)(2,1)S(1)} %get-tuple-element.99.refs_4_.xf_ref.refs_7_) | copy-start | bytes 1572868
  21.5 2.5 %copy-start.2 = (bf16[256,1024]{1,0:T(8,128)(2,1)}, bf16[256,1024]{1,0:T(8,128)(2,1)S(1)}, u32[]{:S(2)}) copy-start(bf16[256,1024]{1,0:T(8,128)(2,1)S(1)} %get-tuple-element.105.refs_5_.xr_ref.refs_8_) | copy-start | bytes 1572868
  21.5 1.1 copy-start.20
  21.5 1.4 copy-start.21
  128.3 29.8 %copy-start.1 = (bf16[256,1024]{1,0:T(8,128)(2,1)S(1)}, bf16[256,1024]{1,0:T(8,128)(2,1)}, u32[]{:S(2)}) copy-start(bf16[256,1024]{1,0:T(8,128)(2,1)} %copy-done) | copy-start | bytes 1572868
  128.3 29.8 %copy-start.3 = (bf16[256,1024]{1,0:T(8,128)(2,1)S(1)}, bf16[256,1024]{1,0:T(8,128)(2,1)}, u32[]{:S(2)}) copy-start(bf16[256,1024]{1,0:T(8,128)(2,1)} %copy-done.2) | copy-start | bytes 1572868
  159.5 1.2 copy-start.5
  159.5 1.5 copy-start.6
  159.5 1.9 copy-start.9
  159.5 2.2 copy-start.10
  163.4 9.3 %collective-permute-start.2 = (f32[3,1024]{1,0:T(4,128)S(1)}, f32[3,1024]{1,0:T(4,128)S(1)}, u32[]{:S(2)}, u32[]{:S(2)}) collective-permute-start(f32[3,1024]{1,0:T(4,128)S(1)} %slice.271), channel_id=1, source_target_pairs={{1,0},{2,1},{3,2},{4,3},{5,4},{6,5},{7,6},{9,8},{10,9},{11,10},{12... | collective-permute-start | bytes 36872 | tf_op jit(solution)/shard_map/ppermute | solution.py:459
  164.7 8.0 %collective-permute-start.3 = (f32[3,1024]{1,0:T(4,128)S(1)}, f32[3,1024]{1,0:T(4,128)S(1)}, u32[]{:S(2)}, u32[]{:S(2)}) collective-permute-start(f32[3,1024]{1,0:T(4,128)S(1)} %slice.274), channel_id=1, source_target_pairs={{0,1},{1,2},{2,3},{3,4},{4,5},{5,6},{6,7},{8,9},{9,10},{10,11},{11... | collective-permute-start | bytes 36872 | tf_op jit(solution)/shard_map/ppermute | solution.py:459
  172.7 0.9 copy-start.11
  172.7 0.9 copy-start.14
  172.7 0.9 copy-start.16
  173.6 8.7 %copy-start.7 = (bf16[256,1024]{1,0:T(8,128)(2,1)}, bf16[256,1024]{1,0:T(8,128)(2,1)S(1)}, u32[]{:S(2)}) copy-start(bf16[256,1024]{1,0:T(8,128)(2,1)S(1)} %fusion.10) | copy-start | bytes 1572868
  173.6 8.7 %copy-start.17 = (f32[1,16]{1,0:T(1,128)S(1)}, f32[1,16]{1,0:T(1,128)}, u32[]{:S(2)}) copy-start(f32[1,16]{1,0:T(1,128)} %get-tuple-element.61) | copy-start | bytes 196
  173.6 8.7 %copy-start.18 = (f32[1,16]{1,0:T(1,128)S(1)}, f32[1,16]{1,0:T(1,128)}, u32[]{:S(2)}) copy-start(f32[1,16]{1,0:T(1,128)} %get-tuple-element.62) | copy-start | bytes 196
  173.6 8.7 %copy-start.19 = (f32[1,16]{1,0:T(1,128)S(1)}, f32[1,16]{1,0:T(1,128)}, u32[]{:S(2)}) copy-start(f32[1,16]{1,0:T(1,128)} %get-tuple-element.63) | copy-start | bytes 196
  225.5 1.5 copy-start.4
  225.5 1.5 copy-start.13
  225.5 2.1 copy-start.8
  227.0 1.7 slice-start
